TPU v7x, 32 devices: a whole 2x2x4 slice. The times are simulated.
32 devices in a mesh: grp: 4 (over y, core), ctx: 8 (over z, x).
Axes of the slice: x: 2, y: 2, z: 4, core: 2. Of those that a mesh axis runs over, the one named last changes fastest.
Arguments:
- query_rows: bfloat16 [4, 1024, 4096], P('grp', 'ctx'), may hold values from -6 to 6
- key_rows: bfloat16 [4, 1024, 512], P('grp', 'ctx'), may hold values from -6 to 6
- value_rows: bfloat16 [4, 1024, 512], P('grp', 'ctx'), may hold values from -5 to 5
- output_rows: bfloat16 [4, 1024, 4096], P('grp', 'ctx'), may hold values from -4 to 4
- output_grad: bfloat16 [4, 1024, 4096], P('grp', 'ctx'), may hold values from -5 to 5
- loss_mask: int32 [4, 1024], P('grp', 'ctx'), may hold values from 0 to 1
- doc_lengths: int32 [4, 12], P('grp'), may hold values from 1 to 256, 1024 in all within a row
- balance_plan: int32 [4, 128], P('grp'), may hold values from 0 to 127, as said below
Outputs:
- query_grad: bfloat16 [4, 1024, 4096], P('grp', 'ctx')
- key_grad: bfloat16 [4, 1024, 512], P('grp', 'ctx')
- value_grad: bfloat16 [4, 1024, 512], P('grp', 'ctx')
Inputs may be any that keep to these rules, and one draw needn't show every extreme that they name: Each row is a permutation of 0 to 127. Span c of a sequence (its tokens c * 8 to c * 8 + 7) goes to index balance_plan // 16 of ctx; of the 16 spans of one index of ctx at most 2 go to the same index.
All inputs are finite; a program needn't handle non-finite values.
Results may differ from a plain program's by a relative error of at most 0.0051.
Values may be sent and summed in bfloat16 or wider, within the bound.
A program may use at most 128 MiB of HBM per device.

v0:
```python
import jax
import jax.numpy as jnp
from jax import lax
from jax.sharding import PartitionSpec as P

HD = 128
QH = 32
KVH = 4
SPAN = 8
NEGATIVE = -1e30


def key_block():
    return 512


def doc_index(positions, doc_ends):
    return jnp.sum((positions[:, None] >= doc_ends[None, :]).astype(jnp.int32), axis=1)


def visible(query_pos, query_doc, key_pos, doc_ends):
    key_doc = doc_index(key_pos, doc_ends)
    return (key_pos[None, :] <= query_pos[:, None]) & (key_doc[None, :] == query_doc[:, None])


def head_scores(q_heads, k_heads, scale_value):
    return (
        jnp.einsum("rgsd,ngd->gsrn", q_heads, k_heads, preferred_element_type=jnp.float32)
        * scale_value
    )


def over_blocks(function, folded, members):
    row_total = members[0].shape[0]
    block_rows = key_block()
    step_count = row_total // block_rows
    stacked = tuple(
        (member.reshape((step_count, block_rows) + member.shape[1:]) for member in members)
    )

    def advance(carried, scanned):
        block_index, pieces = scanned
        positions = block_index * block_rows + jnp.arange(block_rows, dtype=jnp.int32)
        return (function(carried, pieces, positions), None)

    result, unused = lax.scan(advance, folded, (jnp.arange(step_count, dtype=jnp.int32), stacked))
    return result


def stats_update(carried, k_heads, key_pos, context):
    q_heads, query_pos, query_doc, doc_ends, scale_value = context
    old_peak, running_sum = carried
    scores = head_scores(q_heads, k_heads, scale_value)
    visible_mask = visible(query_pos, query_doc, key_pos, doc_ends)
    scores = jnp.where(visible_mask, scores, NEGATIVE)
    new_peak = jnp.maximum(old_peak, jnp.max(scores, axis=-1))
    weights = jnp.where(visible_mask, jnp.exp(scores - new_peak[..., None]), 0.0)
    running_sum = running_sum * jnp.exp(old_peak - new_peak) + jnp.sum(weights, axis=-1)
    return (new_peak, running_sum)


def block_grads(context, k_heads, v_heads, key_pos):
    q_heads, g_heads, query_pos, query_doc, doc_ends, lse_rows, delta_heads, scale_value = context
    scores = head_scores(q_heads, k_heads, scale_value)
    visible_mask = visible(query_pos, query_doc, key_pos, doc_ends)
    probs_full = jnp.where(
        visible_mask, jnp.exp(jnp.where(visible_mask, scores - lse_rows[..., None], NEGATIVE)), 0.0
    )
    probs_half = probs_full.astype(jnp.bfloat16)
    dprobs = jnp.einsum("rgsd,ngd->gsrn", g_heads, v_heads, preferred_element_type=jnp.float32)
    dscores = (probs_full * (dprobs - delta_heads[..., None]) * scale_value).astype(jnp.bfloat16)
    query_part = jnp.einsum("gsrn,ngd->rgsd", dscores, k_heads, preferred_element_type=jnp.float32)
    key_part = jnp.einsum("gsrn,rgsd->ngd", dscores, q_heads, preferred_element_type=jnp.float32)
    value_part = jnp.einsum(
        "gsrn,rgsd->ngd", probs_half, g_heads, preferred_element_type=jnp.float32
    )
    return (query_part, key_part, value_part)


def row_delta(grad_local, output_local):
    local_rows = grad_local.shape[0]
    product = grad_local.astype(jnp.float32) * output_local.astype(jnp.float32)
    return jnp.sum(product.reshape(local_rows, QH, HD), axis=-1)


def shards(
    query_rows, key_rows, value_rows, output_rows, output_grad, loss_mask, doc_lengths, balance_plan
):
    devices = lax.axis_size("ctx")
    device = lax.axis_index("ctx")
    local_rows = query_rows.shape[1]
    per_device = local_rows // SPAN
    slot_count = (per_device + devices - 1) // devices
    group_size = QH // KVH
    scale_value = HD ** (-0.5)
    counted = jnp.sum(loss_mask.astype(jnp.float32))
    total_counted = lax.psum(counted, ("grp", "ctx"))
    factor = lax.axis_size("grp") * devices * local_rows / jnp.maximum(total_counted, 1.0)
    grad_masked = output_grad[0] * loss_mask[0][:, None].astype(jnp.bfloat16)
    plan_row = balance_plan[0]
    dest_all = plan_row // per_device
    dest_grid = dest_all.reshape(devices, per_device)
    earlier = jnp.arange(per_device)[None, :] < jnp.arange(per_device)[:, None]
    same_dest = dest_grid[:, :, None] == dest_grid[:, None, :]
    rank_all = jnp.sum((same_dest & earlier[None, :, :]).astype(jnp.int32), axis=2).reshape(-1)
    inverse = jnp.argsort(plan_row)
    handled = lax.dynamic_slice_in_dim(inverse, device * per_device, per_device)
    receive_index = handled // per_device * slot_count + jnp.take(rank_all, handled)
    send_dest = lax.dynamic_slice_in_dim(dest_all, device * per_device, per_device)
    send_rank = lax.dynamic_slice_in_dim(rank_all, device * per_device, per_device)
    send_index = send_dest * slot_count + send_rank

    def pack_rows(member):
        row_width = member.shape[-1]
        pieces = member.reshape(per_device, SPAN, row_width)
        buffer = jnp.zeros((devices * slot_count, SPAN, row_width), member.dtype)
        return buffer.at[send_index].set(pieces)

    def unpack(member):
        return jnp.take(member, receive_index, axis=0).reshape(local_rows, member.shape[-1])

    moved_query, moved_grad, moved_output = (
        lax.all_to_all(pack_rows(query_rows[0]), "ctx", split_axis=0, concat_axis=0, tiled=True),
        lax.all_to_all(pack_rows(grad_masked), "ctx", split_axis=0, concat_axis=0, tiled=True),
        lax.all_to_all(pack_rows(output_rows[0]), "ctx", split_axis=0, concat_axis=0, tiled=True),
    )
    delta_rows = row_delta(unpack(moved_grad), unpack(moved_output))
    q_local = unpack(moved_query)
    g_local = unpack(moved_grad)
    q_heads = q_local.reshape(local_rows, KVH, group_size, HD)
    g_heads = g_local.reshape(local_rows, KVH, group_size, HD)
    delta_heads = jnp.transpose(delta_rows).reshape(KVH, group_size, local_rows)
    query_pos = (handled[:, None] * SPAN + jnp.arange(SPAN, dtype=jnp.int32)[None, :]).reshape(
        local_rows
    )
    doc_ends = jnp.cumsum(doc_lengths[0])
    query_doc = doc_index(query_pos, doc_ends)
    stats_context = (q_heads, query_pos, query_doc, doc_ends, scale_value)
    stats_initial = (
        jnp.full((KVH, group_size, local_rows), NEGATIVE, jnp.float32),
        jnp.zeros((KVH, group_size, local_rows), jnp.float32),
    )

    def stats_step_rows(carried, members, positions):
        return stats_update(carried, members[0].reshape(-1, KVH, HD), positions, stats_context)

    peak_rows, sum_rows = over_blocks(
        stats_step_rows, stats_initial, (lax.all_gather(key_rows, "ctx", axis=1, tiled=True)[0],)
    )
    lse_rows = peak_rows + jnp.log(sum_rows)
    grad_context = (
        q_heads,
        g_heads,
        query_pos,
        query_doc,
        doc_ends,
        lse_rows,
        delta_heads,
        scale_value,
    )
    dq_zero = jnp.zeros((local_rows, KVH, group_size, HD), jnp.float32)
    seq_total = local_rows * devices
    grads_initial = (
        dq_zero,
        jnp.zeros((seq_total, KVH, HD), jnp.float32),
        jnp.zeros((seq_total, KVH, HD), jnp.float32),
    )

    def grads_step_rows(carried, members, positions):
        dq_acc, dk_all, dv_all = carried
        k_heads = members[0].reshape(-1, KVH, HD)
        v_heads = members[1].reshape(-1, KVH, HD)
        query_part, key_part, value_part = block_grads(grad_context, k_heads, v_heads, positions)
        first_row = positions[0]
        old_keys = lax.dynamic_slice_in_dim(dk_all, first_row, key_part.shape[0], 0)
        dk_all = lax.dynamic_update_slice_in_dim(dk_all, old_keys + key_part, first_row, 0)
        old_values = lax.dynamic_slice_in_dim(dv_all, first_row, value_part.shape[0], 0)
        dv_all = lax.dynamic_update_slice_in_dim(dv_all, old_values + value_part, first_row, 0)
        return (dq_acc + query_part, dk_all, dv_all)

    dq_sum, dk_all, dv_all = over_blocks(
        grads_step_rows,
        grads_initial,
        (
            lax.all_gather(key_rows, "ctx", axis=1, tiled=True)[0],
            lax.all_gather(value_rows, "ctx", axis=1, tiled=True)[0],
        ),
    )
    dk_mine, dv_mine = (
        lax.psum_scatter(dk_all, "ctx", scatter_dimension=0, tiled=True),
        lax.psum_scatter(dv_all, "ctx", scatter_dimension=0, tiled=True),
    )
    query_grad = (dq_sum * factor).astype(jnp.bfloat16).reshape(1, local_rows, QH * HD)
    key_grad = (dk_mine * factor).astype(jnp.bfloat16).reshape(1, local_rows, KVH * HD)
    value_grad = (dv_mine * factor).astype(jnp.bfloat16).reshape(1, local_rows, KVH * HD)
    return (query_grad, key_grad, value_grad)


def solution(mesh):
    in_specs = (
        P("grp", "ctx", None),
        P("grp", "ctx", None),
        P("grp", "ctx", None),
        P("grp", "ctx", None),
        P("grp", "ctx", None),
        P("grp", "ctx"),
        P("grp", None),
        P("grp", None),
    )
    out_specs = (P("grp", "ctx", None), P("grp", "ctx", None), P("grp", "ctx", None))
    return jax.shard_map(shards, mesh=mesh, in_specs=in_specs, out_specs=out_specs, check_vma=False)
```

profile of v0, /device:TPU:0, one launch (start us, length us, event | category | flops | bytes accessed | tf_op | source)
XLA Modules:
  0.0 347.5 jit_solution(4692239312249407797)
XLA Ops:
  8.4 1.3 reduce.7
  11.4 3.4 scatter_fusion
  14.8 7.2 %all-to-all-start = ((bf16[16,8,4096]{2,1,0:T(8,128)(2,1)}), bf16[16,8,4096]{2,1,0:T(8,128)(2,1)S(1)}, u32[]{:S(2)}, u32[]{:S(2)}) async-start(bf16[16,8,4096]{2,1,0:T(8,128)(2,1)} %scatter_fusion), calls=%async_computation | async-start | bytes 2097152 | tf_op jit(solution)/shard_map/all_to_all | solution.py:123
  23.6 1.4 bitcast_multiply_fusion
  26.0 2.9 scatter_fusion.1
  29.0 23.0 %all-to-all-done = bf16[16,8,4096]{2,1,0:T(8,128)(2,1)S(1)} async-done(((bf16[16,8,4096]{2,1,0:T(8,128)(2,1)}), bf16[16,8,4096]{2,1,0:T(8,128)(2,1)S(1)}, u32[]{:S(2)}, u32[]{:S(2)}) %all-to-all-start) | async-done | bytes 1048608 | tf_op jit(solution)/shard_map/all_to_all | solution.py:123
  52.0 4.2 %all-to-all-start.1 = ((bf16[16,8,4096]{2,1,0:T(8,128)(2,1)}), bf16[16,8,4096]{2,1,0:T(8,128)(2,1)}, u32[]{:S(2)}, u32[]{:S(2)}) async-start(bf16[16,8,4096]{2,1,0:T(8,128)(2,1)} %scatter_fusion.1), calls=%async_computation.1 | async-start | bytes 2097152 | tf_op jit(solution)/shard_map/all_to_all | solution.py:124
  57.2 2.5 sort.17
  61.8 3.4 scatter_fusion.2
  65.4 21.0 %all-gather.3.cloned.1.call-done = bf16[1,1024,512]{2,1,0:T(8,128)(2,1)} async-done(((bf16[1,128,512]{2,1,0:T(8,128)(2,1)}), bf16[1,1024,512]{2,1,0:T(8,128)(2,1)}) %all-gather.3.cloned.1.call-update) | async-done | bytes 1048592 | tf_op jit(solution)/shard_map/all_gather | solution.py:185
  86.4 1.5 copy.59
  88.5 1.6 all-to-all-done.1
  90.1 4.2 %all-to-all-start.2 = ((bf16[16,8,4096]{2,1,0:T(8,128)(2,1)}), bf16[16,8,4096]{2,1,0:T(8,128)(2,1)}, u32[]{:S(2)}, u32[]{:S(2)}) async-start(bf16[16,8,4096]{2,1,0:T(8,128)(2,1)} %scatter_fusion.2), calls=%async_computation.2 | async-start | bytes 2097152 | tf_op jit(solution)/shard_map/all_to_all | solution.py:125
  94.4 1.8 gather_fusion.2
  98.1 10.8 %while.28 = (s32[]{:T(128)}, f32[4,8,128]{2,1,0:T(8,128)S(1)}, f32[4,8,128]{2,1,0:T(8,128)S(1)}, s32[2]{0:T(128)S(1)}, s32[12]{0:T(128)S(1)}, /*index=5*/s32[128...) while((s32[]{:T(128)}, f32[4,8,128]{2,1,0:T(8,128)S(1)}, ...), condition=%wide.region_9.11_spmd.clone, body=%wide.region_5.10_spmd.clone.sunk | while | flops 553883776 | bytes 19821336 | solution.py:46
  99.9 1.5 fusion.62
  101.3 2.1 select_reduce_fusion.2
  105.3 1.5 fusion.62
  106.7 2.1 select_reduce_fusion.2
  108.9 1.4 copy.83
  110.3 1.4 copy.62
  111.7 17.6 %all-to-all-done.2 = bf16[16,8,4096]{2,1,0:T(8,128)(2,1)} async-done(((bf16[16,8,4096]{2,1,0:T(8,128)(2,1)}), bf16[16,8,4096]{2,1,0:T(8,128)(2,1)}, u32[]{:S(2)}, u32[]{:S(2)}) %all-to-all-start.2) | async-done | bytes 1048608 | tf_op jit(solution)/shard_map/all_to_all | solution.py:125
  129.3 2.8 gather_fusion.3
  132.2 1.6 multiply_bitcast_fusion
  133.8 1.7 copy.84
  135.5 2.2 reduce_sum.65
  137.8 1.5 broadcast.160.clone
  139.3 1.4 broadcast.160
  140.7 59.4 %while.29 = (s32[]{:T(128)}, f32[128,4,8,128]{0,3,2,1:T(8,128)}, f32[1024,4,128]{2,0,1:T(8,128)}, f32[1024,4,128]{2,0,1:T(8,128)}, bf16[2,512,512]{1,2,0:T(8,128...) while((s32[]{:T(128)}, f32[128,4,8,128]{0,3,2,1:T(8,128)}, ...), condition=%wide.region_15.17_spmd.clone, body=%wide.region_13.16_spmd.clone.sunk | while | flops 2713405440 | bytes 80475096 | solution.py:46
  146.3 1.3 fusion.74
  148.0 3.1 fusion.77
  151.1 3.5 %fusion.75 = bf16[4,8,128,512]{2,3,1,0:T(8,128)(2,1)S(1)} fusion(f32[4,512,128,8]{2,1,3,0:T(8,128)S(1)} %fusion.74, f32[4,8,128]{2,1,0:T(8,128)S(1)} %bitcast.176, f32[4,8,128]{2,1,0:T(8,128)S(1)} %get-tuple-element.587, pred[128,512]{0,1:T(8,128)(4,1)S(1)} %compare_and_fusion.6, bf16[512,4,128,1]{0,2,3,1:T(8,128)(2,1)S(1)} %bitcast.164, ...), kind=kOutput, calls=%fused_computation.23.clone.1 | convolution fusion | flops 553648128 | bytes 14254080 | tf_op jit(solution)/shard_map/while/body/eval_jaxpr/rgsd,ngd->gsrn/dot_general | solution.py:70
  154.7 1.3 fusion.76
  156.0 2.3 bitcast_add_fusion.2
  158.2 5.9 %dynamic_update_slice.10 = f32[1024,4,128]{2,0,1:T(8,128)} dynamic-update-slice(f32[1024,4,128]{2,0,1:T(8,128)} %get-tuple-element.562, f32[512,4,128]{2,0,1:T(8,128)S(1)} %fusion.76, s32[]{:T(128)S(6)} %select_n.158, s32[]{:T(128)} %constant.75.clone.1..sunk.1, s32[]{:T(128)} %constant.75.clone.1..sunk.1) | dynamic-update-slice | bytes 2097156 | tf_op jit(solution)/shard_map/while/body/eval_jaxpr/dynamic_update_slice | solution.py:176
  164.1 6.2 %dynamic_update_slice.11 = f32[1024,4,128]{2,0,1:T(8,128)} dynamic-update-slice(f32[1024,4,128]{2,0,1:T(8,128)} %get-tuple-element.563, f32[512,4,128]{2,0,1:T(8,128)} %fusion.77, s32[]{:T(128)S(6)} %select_n.158, s32[]{:T(128)} %constant.75.clone.1..sunk.1, s32[]{:T(128)} %constant.75.clone.1..sunk.1) | dynamic-update-slice | bytes 2097156 | tf_op jit(solution)/shard_map/while/body/eval_jaxpr/dynamic_update_slice | solution.py:178
  175.9 1.3 fusion.74
  177.7 3.1 fusion.77
  180.7 3.5 %fusion.75 = bf16[4,8,128,512]{2,3,1,0:T(8,128)(2,1)S(1)} fusion(f32[4,512,128,8]{2,1,3,0:T(8,128)S(1)} %fusion.74, f32[4,8,128]{2,1,0:T(8,128)S(1)} %bitcast.176, f32[4,8,128]{2,1,0:T(8,128)S(1)} %get-tuple-element.587, pred[128,512]{0,1:T(8,128)(4,1)S(1)} %compare_and_fusion.6, bf16[512,4,128,1]{0,2,3,1:T(8,128)(2,1)S(1)} %bitcast.164, ...), kind=kOutput, calls=%fused_computation.23.clone.1 | convolution fusion | flops 553648128 | bytes 14254080 | tf_op jit(solution)/shard_map/while/body/eval_jaxpr/rgsd,ngd->gsrn/dot_general | solution.py:70
  184.3 1.3 fusion.76
  185.6 3.9 %bitcast_add_fusion.2 = f32[128,4,8,128]{0,3,2,1:T(8,128)} fusion(f32[128,4,8,128]{0,3,2,1:T(8,128)} %get-tuple-element.561, bf16[512,4,128,1]{0,2,3,1:T(8,128)(2,1)S(1)} %bitcast.162, bf16[4,8,128,512]{2,3,1,0:T(8,128)(2,1)S(1)} %fusion.75, pred[]{:T(512)S(6)} %compare.25), kind=kOutput, calls=%fused_computation.31.clone.1 | convolution fusion | flops 537919488 | bytes 8912897 | tf_op jit(solution)/shard_map/while/body/eval_jaxpr/gsrn,ngd->rgsd/dot_general | solution.py:72
  189.4 5.2 %dynamic_update_slice.10 = f32[1024,4,128]{2,0,1:T(8,128)} dynamic-update-slice(f32[1024,4,128]{2,0,1:T(8,128)} %get-tuple-element.562, f32[512,4,128]{2,0,1:T(8,128)S(1)} %fusion.76, s32[]{:T(128)S(6)} %select_n.158, s32[]{:T(128)} %constant.75.clone.1..sunk.1, s32[]{:T(128)} %constant.75.clone.1..sunk.1) | dynamic-update-slice | bytes 2097156 | tf_op jit(solution)/shard_map/while/body/eval_jaxpr/dynamic_update_slice | solution.py:176
  194.6 5.5 %dynamic_update_slice.11 = f32[1024,4,128]{2,0,1:T(8,128)} dynamic-update-slice(f32[1024,4,128]{2,0,1:T(8,128)} %get-tuple-element.563, f32[512,4,128]{2,0,1:T(8,128)} %fusion.77, s32[]{:T(128)S(6)} %select_n.158, s32[]{:T(128)} %constant.75.clone.1..sunk.1, s32[]{:T(128)} %constant.75.clone.1..sunk.1) | dynamic-update-slice | bytes 2097156 | tf_op jit(solution)/shard_map/while/body/eval_jaxpr/dynamic_update_slice | solution.py:178
  201.4 40.0 %psum.7 = f32[]{:T(128)} all-reduce(f32[]{:T(128)} %convert_reduce_fusion.4), channel_id=1, replica_groups=mesh['grp'=4,'ctx'=8] {'grp','ctx'}, use_global_device_ids=true, to_apply=%region_17.19 | all-reduce | flops 1 | bytes 8 | tf_op jit(solution)/shard_map/psum | solution.py:97
  242.0 1.9 multiply_convert_fusion
  243.9 1.3 copy.74
  245.2 22.4 %reduce-scatter.5.cloned.1.call-done = f32[128,4,128]{2,0,1:T(8,128)} async-done(((f32[1024,4,128]{2,0,1:T(8,128)}), f32[128,4,128]{2,0,1:T(8,128)}) %reduce-scatter.5.cloned.1.call-update) | async-done | bytes 262160 | tf_op jit(solution)/shard_map/reduce_scatter | solution.py:191
  267.6 70.6 %reduce-scatter.3.cloned.1.call-done = f32[128,4,128]{2,0,1:T(8,128)} async-done(((f32[1024,4,128]{2,0,1:T(8,128)}), f32[128,4,128]{2,0,1:T(8,128)}) %reduce-scatter.3.cloned.1.call-update) | async-done | bytes 262160 | tf_op jit(solution)/shard_map/reduce_scatter | solution.py:190
  (107 shorter events, 24.1 us)
Async XLA Ops:
  7.2 50.1 %copy-start.4 = (s32[1,128]{1,0:T(1,128)S(1)}, s32[1,128]{1,0:T(1,128)}, u32[]{:S(2)}) copy-start(s32[1,128]{1,0:T(1,128)} %param.21) | copy-start | bytes 1540
  7.2 49.9 %copy-start.3 = (s32[1,12]{1,0:T(1,128)S(1)}, s32[1,12]{1,0:T(1,128)}, u32[]{:S(2)}) copy-start(s32[1,12]{1,0:T(1,128)} %param.20) | copy-start | bytes 148
  14.8 37.2 %all-to-all-start = ((bf16[16,8,4096]{2,1,0:T(8,128)(2,1)}), bf16[16,8,4096]{2,1,0:T(8,128)(2,1)S(1)}, u32[]{:S(2)}, u32[]{:S(2)}) async-start(bf16[16,8,4096]{2,1,0:T(8,128)(2,1)} %scatter_fusion), calls=%async_computation | async-start | bytes 2097152 | tf_op jit(solution)/shard_map/all_to_all | solution.py:123
  22.1 64.3 %all-gather.3.cloned.1.call-start = ((), (), s32[]{:S(2)}) async-start(), calls=%async_computation.5 | async-start | bytes 1179648 | tf_op jit(solution)/shard_map/all_gather | solution.py:185
  52.0 38.1 %all-to-all-start.1 = ((bf16[16,8,4096]{2,1,0:T(8,128)(2,1)}), bf16[16,8,4096]{2,1,0:T(8,128)(2,1)}, u32[]{:S(2)}, u32[]{:S(2)}) async-start(bf16[16,8,4096]{2,1,0:T(8,128)(2,1)} %scatter_fusion.1), calls=%async_computation.1 | async-start | bytes 2097152 | tf_op jit(solution)/shard_map/all_to_all | solution.py:124
  56.3 81.5 %all-gather.5.cloned.1.call-start = ((), (), s32[]{:S(2)}) async-start(), calls=%async_computation.6 | async-start | bytes 1179648 | tf_op jit(solution)/shard_map/all_gather | solution.py:186
  90.1 39.3 %all-to-all-start.2 = ((bf16[16,8,4096]{2,1,0:T(8,128)(2,1)}), bf16[16,8,4096]{2,1,0:T(8,128)(2,1)}, u32[]{:S(2)}, u32[]{:S(2)}) async-start(bf16[16,8,4096]{2,1,0:T(8,128)(2,1)} %scatter_fusion.2), calls=%async_computation.2 | async-start | bytes 2097152 | tf_op jit(solution)/shard_map/all_to_all | solution.py:125
  94.3 173.3 %reduce-scatter.5.cloned.1.call-start = ((), (), s32[]{:S(2)}) async-start(), calls=%async_computation.8 | async-start | bytes 2359296 | tf_op jit(solution)/shard_map/reduce_scatter | solution.py:191
  140.7 60.0 %copy-start.5 = (s32[1,128]{1,0:T(1,128)S(1)}, s32[1,128]{1,0:T(1,128)}, u32[]{:S(2)}) copy-start(s32[1,128]{1,0:T(1,128)} %param.19) | copy-start | bytes 1540
  146.2 1.6 copy-start.1
  146.2 1.8 copy-start.2
  151.1 3.6 %copy-start = (f32[1024,4,128]{2,0,1:T(8,128)S(1)}, f32[1024,4,128]{2,0,1:T(8,128)}, u32[]{:S(2)}) copy-start(f32[1024,4,128]{2,0,1:T(8,128)} %get-tuple-element.562) | copy-start | bytes 6291460 | tf_op jit(solution)/shard_map/while
  175.8 1.6 copy-start.1
  175.8 1.8 copy-start.2
  180.7 3.6 %copy-start = (f32[1024,4,128]{2,0,1:T(8,128)S(1)}, f32[1024,4,128]{2,0,1:T(8,128)}, u32[]{:S(2)}) copy-start(f32[1024,4,128]{2,0,1:T(8,128)} %get-tuple-element.562) | copy-start | bytes 6291460 | tf_op jit(solution)/shard_map/while
  200.2 138.1 %reduce-scatter.3.cloned.1.call-start = ((), (), s32[]{:S(2)}) async-start(), calls=%async_computation.7 | async-start | bytes 2359296 | tf_op jit(solution)/shard_map/reduce_scatter | solution.py:190
Sparse Core Ops, SparseCore 0:
  25.0 61.2 all-gather.2
  88.5 45.8 all-gather.4
  200.3 67.3 reduce-scatter.4
  271.0 67.1 reduce-scatter.2
where the time goes:
time: 349 us; the launch traced here: 347 us
  waiting for transfers between devices  158 us (45%)
  local copies, waits for them, and re-layouts  62.7 us (18%)
  blocking collectives  40 us (11%)
  matrix products  27.4 us (8%)
  other arithmetic  21.9 us (6%)
  starting transfers between devices  15.9 us (5%)
  between operations  14.7 us (4%)
  loops' own time  6.75 us (2%)
    reduce_scatter x1, waiting for transfers between devices, shards(): lax.psum_scatter(dk_all, 'ctx', scatter_dimension=0, tiled=True)  70.6 us
    psum x1, blocking collectives, shards(): total_counted = lax.psum(counted, ('grp', 'ctx'))  40 us
    all_to_all x1, waiting for transfers between devices, shards(): lax.all_to_all(pack_rows(query_rows[0]), 'ctx', split_axis=0, concat_axis...  23 us
    reduce_scatter x1, waiting for transfers between devices, shards(): lax.psum_scatter(dv_all, 'ctx', scatter_dimension=0, tiled=True)  22.4 us
    all_gather x1, waiting for transfers between devices, shards(): lax.all_gather(key_rows, 'ctx', axis=1, tiled=True)[0]  21 us
    all_to_all x1, waiting for transfers between devices, shards(): lax.all_to_all(pack_rows(output_rows[0]), 'ctx', split_axis=0, concat_axi...  17.6 us
    dynamic_update_slice x2, local copies, waits for them, and re-layouts, grads_step_rows(): lax.dynamic_update_slice_in_dim(dv_all, old_values + value_part, first_ro...  11.7 us
    dynamic_update_slice x2, local copies, waits for them, and re-layouts, grads_step_rows(): lax.dynamic_update_slice_in_dim(dk_all, old_keys + key_part, first_row, 0)  11.1 us
  transfers between devices with their start and end apart: 7, of which 6 were waited for; matrix products, arithmetic and copies ran while one was open for 13% of the time, Pallas kernels for 0%

commit v1 on v0

--- a/solution.py
+++ b/solution.py
@@ -8,6 +8,30 @@
 KVH = 4
 SPAN = 8
 NEGATIVE = -1e30
+
+
+def cut_along(x, dim, size):
+    before, after = (x.shape[:dim], x.shape[dim + 1 :])
+    return jnp.moveaxis(x.reshape(*before, size, -1, *after), dim, 0)
+
+
+def laid_out(parts, dim):
+    shape = list(parts.shape[1:])
+    shape[dim] *= parts.shape[0]
+    return jnp.moveaxis(parts, 0, dim).reshape(shape)
+
+
+def sent_to_each(array, axis, split_dim, concat_dim):
+    devices, index = (lax.axis_size(axis), lax.axis_index(axis))
+    tiles = cut_along(array, split_dim, devices)
+    gathered = [tiles[index]]
+    for step in range(1, devices):
+        sent = tiles[(index + step) % devices]
+        gathered.append(
+            lax.ppermute(sent, axis, [(i, (i + step) % devices) for i in range(devices)])
+        )
+    tiles = jnp.stack(gathered)[(index - jnp.arange(devices)) % devices]
+    return laid_out(tiles, concat_dim)
 
 
 def key_block():
@@ -122,7 +146,7 @@
     moved_query, moved_grad, moved_output = (
         lax.all_to_all(pack_rows(query_rows[0]), "ctx", split_axis=0, concat_axis=0, tiled=True),
         lax.all_to_all(pack_rows(grad_masked), "ctx", split_axis=0, concat_axis=0, tiled=True),
-        lax.all_to_all(pack_rows(output_rows[0]), "ctx", split_axis=0, concat_axis=0, tiled=True),
+        sent_to_each(pack_rows(output_rows[0]), "ctx", 0, 0),
     )
     delta_rows = row_delta(unpack(moved_grad), unpack(moved_output))
     q_local = unpack(moved_query)

time: 349 us -> 367 us (1.052)
  starting transfers between devices: 15.9 us -> 36.1 us
  waiting for transfers between devices: 158 us -> 150 us
  local copies, waits for them, and re-layouts: 62.7 us -> 69.2 us
    ppermute x0 -> x7, waiting for transfers between devices: none -> 28.7 us  [sent_to_each(): lax.ppermute(sent, axis, [(i, (i + step) % devices) for i in range(device...]
    all_to_all x1, waiting for transfers between devices: 1.56 us -> 25.7 us  [shards(): lax.all_to_all(pack_rows(grad_masked), 'ctx', split_axis=0, concat_axis=0...]
    all_to_all x1, waiting for transfers between devices: 23 us -> 0.01 us  [shards(): lax.all_to_all(pack_rows(query_rows[0]), 'ctx', split_axis=0, concat_axis...]
    all_gather x1, waiting for transfers between devices: 21 us -> 0.01 us  [shards(): lax.all_gather(key_rows, 'ctx', axis=1, tiled=True)[0]]
    all_to_all x1 -> x0, waiting for transfers between devices: 17.6 us -> none  [shards(): lax.all_to_all(pack_rows(output_rows[0]), 'ctx', split_axis=0, concat_axi...]
    ppermute x0 -> x7, starting transfers between devices: none -> 16 us  [sent_to_each(): lax.ppermute(sent, axis, [(i, (i + step) % devices) for i in range(device...]
    all_to_all x1, starting transfers between devices: 4.25 us -> 12.7 us  [shards(): lax.all_to_all(pack_rows(grad_masked), 'ctx', split_axis=0, concat_axis=0...]
    unnamed x14 -> x22, local copies, waits for them, and re-layouts: 7.21 us -> 13.9 us
  transfers between devices with their start and end apart: 7 -> 13, of which waited for: 6 -> 6; matrix products, arithmetic and copies ran while one was open for 13% -> 16% of each run, Pallas kernels for 0% -> 0%
where the time goes in v1:
time: 367 us; the launch traced here: 365 us
  waiting for transfers between devices  150 us (41%)
  local copies, waits for them, and re-layouts  69.2 us (19%)
  blocking collectives  39.5 us (11%)
  starting transfers between devices  36.1 us (10%)
  matrix products  27.4 us (7%)
  other arithmetic  21.2 us (6%)
  between operations  14.9 us (4%)
  loops' own time  6.79 us (2%)
    reduce_scatter x1, waiting for transfers between devices, shards(): lax.psum_scatter(dk_all, 'ctx', scatter_dimension=0, tiled=True)  70.6 us
    psum x1, blocking collectives, shards(): total_counted = lax.psum(counted, ('grp', 'ctx'))  39.5 us
    ppermute x7, waiting for transfers between devices, sent_to_each(): lax.ppermute(sent, axis, [(i, (i + step) % devices) for i in range(device...  28.7 us
    all_to_all x1, waiting for transfers between devices, shards(): lax.all_to_all(pack_rows(grad_masked), 'ctx', split_axis=0, concat_axis=0...  25.7 us
    reduce_scatter x1, waiting for transfers between devices, shards(): lax.psum_scatter(dv_all, 'ctx', scatter_dimension=0, tiled=True)  24 us
    ppermute x7, starting transfers between devices, sent_to_each(): lax.ppermute(sent, axis, [(i, (i + step) % devices) for i in range(device...  16 us
    unnamed x22, local copies, waits for them, and re-layouts  13.9 us
    all_to_all x1, starting transfers between devices, shards(): lax.all_to_all(pack_rows(grad_masked), 'ctx', split_axis=0, concat_axis=0...  12.7 us
  transfers between devices with their start and end apart: 13, of which 6 were waited for; matrix products, arithmetic and copies ran while one was open for 16% of the time, Pallas kernels for 0%

profile of v1, /device:TPU:0, one launch (start us, length us, event | category | flops | bytes accessed | tf_op | source)
XLA Modules:
  0.0 365.4 jit_solution(10974402095410260075)
XLA Ops:
  12.1 3.4 scatter_fusion
  15.5 7.2 %all-to-all-start = ((bf16[16,8,4096]{2,1,0:T(8,128)(2,1)}), bf16[16,8,4096]{2,1,0:T(8,128)(2,1)S(1)}, u32[]{:S(2)}, u32[]{:S(2)}) async-start(bf16[16,8,4096]{2,1,0:T(8,128)(2,1)} %scatter_fusion), calls=%async_computation | async-start | bytes 2097152 | tf_op jit(solution)/shard_map/all_to_all | solution.py:147
  23.0 2.3 scatter_fusion.2
  26.0 4.6 %collective-permute-start.6 = (bf16[2,8,4096]{2,1,0:T(8,128)(2,1)S(1)}, bf16[2,8,4096]{2,1,0:T(8,128)(2,1)S(1)}, u32[]{:S(2)}, u32[]{:S(2)}) collective-permute-start(bf16[2,8,4096]{2,1,0:T(8,128)(2,1)S(1)} %get-tuple-element.356), channel_id=1, source_target_pairs={{0,7},{1,0},{2,1},{3,2},{4,3},{5,4},{6,5},{7,6},{8,15},{9,8},{10,9... | collective-permute-start | bytes 393224 | tf_op jit(solution)/shard_map/ppermute | solution.py:31
  31.2 2.9 collective-permute-start.3
  34.1 1.5 collective-permute-start
  35.6 2.5 sort.17
  42.0 2.9 scatter_fusion.1
  45.0 20.7 %collective-permute-done = bf16[2,8,4096]{2,1,0:T(8,128)(2,1)} collective-permute-done((bf16[2,8,4096]{2,1,0:T(8,128)(2,1)S(1)}, bf16[2,8,4096]{2,1,0:T(8,128)(2,1)}, u32[]{:S(2)}, u32[]{:S(2)}) %collective-permute-start) | collective-permute-done | bytes 131104 | tf_op jit(solution)/shard_map/ppermute | solution.py:31
  66.0 1.5 bitcast_dynamic-update-slice_fusion.6
  67.5 5.1 %collective-permute-done.1 = bf16[2,8,4096]{2,1,0:T(8,128)(2,1)S(1)} collective-permute-done((bf16[2,8,4096]{2,1,0:T(8,128)(2,1)S(1)}, bf16[2,8,4096]{2,1,0:T(8,128)(2,1)S(1)}, u32[]{:S(2)}, u32[]{:S(2)}) %collective-permute-start.1) | collective-permute-done | bytes 131104 | tf_op jit(solution)/shard_map/ppermute | solution.py:31
  72.6 6.1 %collective-permute-start.2 = (bf16[2,8,4096]{2,1,0:T(8,128)(2,1)S(1)}, bf16[2,8,4096]{2,1,0:T(8,128)(2,1)S(1)}, u32[]{:S(2)}, u32[]{:S(2)}) collective-permute-start(bf16[2,8,4096]{2,1,0:T(8,128)(2,1)S(1)} %get-tuple-element.360), channel_id=1, source_target_pairs={{0,3},{1,4},{2,5},{3,6},{4,7},{5,0},{6,1},{7,2},{8,11},{9,12},{10,... | collective-permute-start | bytes 393224 | tf_op jit(solution)/shard_map/ppermute | solution.py:31
  79.5 3.0 collective-permute-done.2
  83.1 1.6 bitcast_dynamic-update-slice_fusion.3
  84.6 12.7 %all-to-all-start.1 = ((bf16[16,8,4096]{2,1,0:T(8,128)(2,1)}), bf16[16,8,4096]{2,1,0:T(8,128)(2,1)}, u32[]{:S(2)}, u32[]{:S(2)}) async-start(bf16[16,8,4096]{2,1,0:T(8,128)(2,1)} %scatter_fusion.1), calls=%async_computation.1 | async-start | bytes 2097152 | tf_op jit(solution)/shard_map/all_to_all | solution.py:148
  97.4 1.6 bitcast_dynamic-update-slice_fusion.2
  100.3 1.8 gather_fusion.1
  102.1 1.6 gather_fusion.4
  103.7 1.5 copy.59
  105.9 25.7 %all-to-all-done.1 = bf16[16,8,4096]{2,1,0:T(8,128)(2,1)} async-done(((bf16[16,8,4096]{2,1,0:T(8,128)(2,1)}), bf16[16,8,4096]{2,1,0:T(8,128)(2,1)}, u32[]{:S(2)}, u32[]{:S(2)}) %all-to-all-start.1) | async-done | bytes 1048608 | tf_op jit(solution)/shard_map/all_to_all | solution.py:148
  131.5 1.8 gather_fusion.3
  135.3 10.8 %while.28 = (s32[]{:T(128)}, f32[4,8,128]{2,1,0:T(8,128)S(1)}, f32[4,8,128]{2,1,0:T(8,128)S(1)}, s32[2]{0:T(128)S(1)}, s32[12]{0:T(128)S(1)}, /*index=5*/s32[128...) while((s32[]{:T(128)}, f32[4,8,128]{2,1,0:T(8,128)S(1)}, ...), condition=%wide.region_9.11_spmd.clone, body=%wide.region_5.10_spmd.clone.sunk | while | flops 553883776 | bytes 19821336 | solution.py:70
  137.1 1.5 fusion.64
  138.6 2.1 select_reduce_fusion.2
  142.5 1.5 fusion.64
  144.0 2.1 select_reduce_fusion.2
  146.1 1.4 copy.83
  147.6 1.4 copy.62
  149.0 1.6 multiply_bitcast_fusion
  150.6 1.7 copy.84
  152.3 2.2 reduce_sum.65
  154.6 1.5 broadcast.236.clone
  156.1 1.4 broadcast.236
  157.5 59.4 %while.29 = (s32[]{:T(128)}, f32[128,4,8,128]{0,3,2,1:T(8,128)}, f32[1024,4,128]{2,0,1:T(8,128)}, f32[1024,4,128]{2,0,1:T(8,128)}, bf16[2,512,512]{1,2,0:T(8,128...) while((s32[]{:T(128)}, f32[128,4,8,128]{0,3,2,1:T(8,128)}, ...), condition=%wide.region_15.17_spmd.clone, body=%wide.region_13.16_spmd.clone.sunk | while | flops 2713405440 | bytes 80475096 | solution.py:70
  164.8 3.1 fusion.79
  167.9 3.5 fusion.77
  172.7 2.3 bitcast_add_fusion.2
  175.0 5.9 %dynamic_update_slice.10 = f32[1024,4,128]{2,0,1:T(8,128)} dynamic-update-slice(f32[1024,4,128]{2,0,1:T(8,128)} %get-tuple-element.570, f32[512,4,128]{2,0,1:T(8,128)S(1)} %fusion.78, s32[]{:T(128)S(6)} %select_n.261, s32[]{:T(128)} %constant.151.clone.1..sunk.1, s32[]{:T(128)} %constant.151.clone.1..sunk.1) | dynamic-update-slice | bytes 2097156 | tf_op jit(solution)/shard_map/while/body/eval_jaxpr/dynamic_update_slice | solution.py:200
  180.9 6.2 %dynamic_update_slice.11 = f32[1024,4,128]{2,0,1:T(8,128)} dynamic-update-slice(f32[1024,4,128]{2,0,1:T(8,128)} %get-tuple-element.571, f32[512,4,128]{2,0,1:T(8,128)} %fusion.79, s32[]{:T(128)S(6)} %select_n.261, s32[]{:T(128)} %constant.151.clone.1..sunk.1, s32[]{:T(128)} %constant.151.clone.1..sunk.1) | dynamic-update-slice | bytes 2097156 | tf_op jit(solution)/shard_map/while/body/eval_jaxpr/dynamic_update_slice | solution.py:202
  194.4 3.1 fusion.79
  197.5 3.5 fusion.77
  202.3 3.9 %bitcast_add_fusion.2 = f32[128,4,8,128]{0,3,2,1:T(8,128)} fusion(f32[128,4,8,128]{0,3,2,1:T(8,128)} %get-tuple-element.569, bf16[512,4,128,1]{0,2,3,1:T(8,128)(2,1)S(1)} %bitcast.194, bf16[4,8,128,512]{2,3,1,0:T(8,128)(2,1)S(1)} %fusion.77, pred[]{:T(512)S(6)} %compare.39), kind=kOutput, calls=%fused_computation.32.clone.1 | convolution fusion | flops 537919488 | bytes 8912897 | tf_op jit(solution)/shard_map/while/body/eval_jaxpr/gsrn,ngd->rgsd/dot_general | solution.py:96
  206.2 5.2 %dynamic_update_slice.10 = f32[1024,4,128]{2,0,1:T(8,128)} dynamic-update-slice(f32[1024,4,128]{2,0,1:T(8,128)} %get-tuple-element.570, f32[512,4,128]{2,0,1:T(8,128)S(1)} %fusion.78, s32[]{:T(128)S(6)} %select_n.261, s32[]{:T(128)} %constant.151.clone.1..sunk.1, s32[]{:T(128)} %constant.151.clone.1..sunk.1) | dynamic-update-slice | bytes 2097156 | tf_op jit(solution)/shard_map/while/body/eval_jaxpr/dynamic_update_slice | solution.py:200
  211.4 5.5 %dynamic_update_slice.11 = f32[1024,4,128]{2,0,1:T(8,128)} dynamic-update-slice(f32[1024,4,128]{2,0,1:T(8,128)} %get-tuple-element.571, f32[512,4,128]{2,0,1:T(8,128)} %fusion.79, s32[]{:T(128)S(6)} %select_n.261, s32[]{:T(128)} %constant.151.clone.1..sunk.1, s32[]{:T(128)} %constant.151.clone.1..sunk.1) | dynamic-update-slice | bytes 2097156 | tf_op jit(solution)/shard_map/while/body/eval_jaxpr/dynamic_update_slice | solution.py:202
  218.1 39.5 %psum.7 = f32[]{:T(128)} all-reduce(f32[]{:T(128)} %convert_reduce_fusion.4), channel_id=1, replica_groups=mesh['grp'=4,'ctx'=8] {'grp','ctx'}, use_global_device_ids=true, to_apply=%region_17.19 | all-reduce | flops 1 | bytes 8 | tf_op jit(solution)/shard_map/psum | solution.py:121
  258.3 1.9 multiply_convert_fusion
  261.5 24.0 %reduce-scatter.5.cloned.1.call-done = f32[128,4,128]{2,0,1:T(8,128)} async-done(((f32[1024,4,128]{2,0,1:T(8,128)}), f32[128,4,128]{2,0,1:T(8,128)}) %reduce-scatter.5.cloned.1.call-update) | async-done | bytes 262160 | tf_op jit(solution)/shard_map/reduce_scatter | solution.py:215
  285.6 70.6 %reduce-scatter.3.cloned.1.call-done = f32[128,4,128]{2,0,1:T(8,128)} async-done(((f32[1024,4,128]{2,0,1:T(8,128)}), f32[128,4,128]{2,0,1:T(8,128)}) %reduce-scatter.3.cloned.1.call-update) | async-done | bytes 262160 | tf_op jit(solution)/shard_map/reduce_scatter | solution.py:214
  (132 shorter events, 35.2 us)
Async XLA Ops:
  7.2 28.5 %copy-start.3 = (s32[1,128]{1,0:T(1,128)S(1)}, s32[1,128]{1,0:T(1,128)}, u32[]{:S(2)}) copy-start(s32[1,128]{1,0:T(1,128)} %param.21) | copy-start | bytes 1540
  7.2 28.4 %copy-start.5 = (s32[1,128]{1,0:T(1,128)S(1)}, s32[1,128]{1,0:T(1,128)}, u32[]{:S(2)}) copy-start(s32[1,128]{1,0:T(1,128)} %param.19) | copy-start | bytes 1540
  7.2 33.4 %copy-start.4 = (s32[1,12]{1,0:T(1,128)S(1)}, s32[1,12]{1,0:T(1,128)}, u32[]{:S(2)}) copy-start(s32[1,12]{1,0:T(1,128)} %param.20) | copy-start | bytes 148
  7.2 96.5 %all-gather.3.cloned.1.call-start = ((), (), s32[]{:S(2)}) async-start(), calls=%async_computation.4 | async-start | bytes 1179648 | tf_op jit(solution)/shard_map/all_gather | solution.py:209
  15.5 69.1 %all-to-all-start = ((bf16[16,8,4096]{2,1,0:T(8,128)(2,1)}), bf16[16,8,4096]{2,1,0:T(8,128)(2,1)S(1)}, u32[]{:S(2)}, u32[]{:S(2)}) async-start(bf16[16,8,4096]{2,1,0:T(8,128)(2,1)} %scatter_fusion), calls=%async_computation | async-start | bytes 2097152 | tf_op jit(solution)/shard_map/all_to_all | solution.py:147
  22.7 131.9 %all-gather.5.cloned.1.call-start = ((), (), s32[]{:S(2)}) async-start(), calls=%async_computation.5 | async-start | bytes 1179648 | tf_op jit(solution)/shard_map/all_gather | solution.py:210
  26.0 73.6 %collective-permute-start.6 = (bf16[2,8,4096]{2,1,0:T(8,128)(2,1)S(1)}, bf16[2,8,4096]{2,1,0:T(8,128)(2,1)S(1)}, u32[]{:S(2)}, u32[]{:S(2)}) collective-permute-start(bf16[2,8,4096]{2,1,0:T(8,128)(2,1)S(1)} %get-tuple-element.356), channel_id=1, source_target_pairs={{0,7},{1,0},{2,1},{3,2},{4,3},{5,4},{6,5},{7,6},{8,15},{9,8},{10,9... | collective-permute-start | bytes 393224 | tf_op jit(solution)/shard_map/ppermute | solution.py:31
  30.6 68.4 %collective-permute-start.5 = (bf16[2,8,4096]{2,1,0:T(8,128)(2,1)S(1)}, bf16[2,8,4096]{2,1,0:T(8,128)(2,1)S(1)}, u32[]{:S(2)}, u32[]{:S(2)}) collective-permute-start(bf16[2,8,4096]{2,1,0:T(8,128)(2,1)S(1)} %get-tuple-element.357), channel_id=1, source_target_pairs={{0,6},{1,7},{2,0},{3,1},{4,2},{5,3},{6,4},{7,5},{8,14},{9,15},{10,... | collective-permute-start | bytes 393224 | tf_op jit(solution)/shard_map/ppermute | solution.py:31
  31.2 66.2 %collective-permute-start.4 = (bf16[2,8,4096]{2,1,0:T(8,128)(2,1)S(1)}, bf16[2,8,4096]{2,1,0:T(8,128)(2,1)}, u32[]{:S(2)}, u32[]{:S(2)}) collective-permute-start(bf16[2,8,4096]{2,1,0:T(8,128)(2,1)S(1)} %get-tuple-element.358), channel_id=1, source_target_pairs={{0,5},{1,6},{2,7},{3,0},{4,1},{5,2},{6,3},{7,4},{8,13},{9,14},{10,... | collective-permute-start | bytes 393224 | tf_op jit(solution)/shard_map/ppermute | solution.py:31
  31.2 51.9 %collective-permute-start.3 = (bf16[2,8,4096]{2,1,0:T(8,128)(2,1)S(1)}, bf16[2,8,4096]{2,1,0:T(8,128)(2,1)}, u32[]{:S(2)}, u32[]{:S(2)}) collective-permute-start(bf16[2,8,4096]{2,1,0:T(8,128)(2,1)S(1)} %get-tuple-element.359), channel_id=1, source_target_pairs={{0,4},{1,5},{2,6},{3,7},{4,0},{5,1},{6,2},{7,3},{8,12},{9,13},{10,... | collective-permute-start | bytes 393224 | tf_op jit(solution)/shard_map/ppermute | solution.py:31
  34.1 31.6 %collective-permute-start = (bf16[2,8,4096]{2,1,0:T(8,128)(2,1)S(1)}, bf16[2,8,4096]{2,1,0:T(8,128)(2,1)}, u32[]{:S(2)}, u32[]{:S(2)}) collective-permute-start(bf16[2,8,4096]{2,1,0:T(8,128)(2,1)S(1)} %get-tuple-element.362), channel_id=1, source_target_pairs={{0,1},{1,2},{2,3},{3,4},{4,5},{5,6},{6,7},{7,0},{8,9},{9,10},{10,1... | collective-permute-start | bytes 393224 | tf_op jit(solution)/shard_map/ppermute | solution.py:31
  65.7 7.0 %collective-permute-start.1 = (bf16[2,8,4096]{2,1,0:T(8,128)(2,1)S(1)}, bf16[2,8,4096]{2,1,0:T(8,128)(2,1)S(1)}, u32[]{:S(2)}, u32[]{:S(2)}) collective-permute-start(bf16[2,8,4096]{2,1,0:T(8,128)(2,1)S(1)} %get-tuple-element.361), channel_id=1, source_target_pairs={{0,2},{1,3},{2,4},{3,5},{4,6},{5,7},{6,0},{7,1},{8,10},{9,11},{10,... | collective-permute-start | bytes 393224 | tf_op jit(solution)/shard_map/ppermute | solution.py:31
  72.6 9.8 %collective-permute-start.2 = (bf16[2,8,4096]{2,1,0:T(8,128)(2,1)S(1)}, bf16[2,8,4096]{2,1,0:T(8,128)(2,1)S(1)}, u32[]{:S(2)}, u32[]{:S(2)}) collective-permute-start(bf16[2,8,4096]{2,1,0:T(8,128)(2,1)S(1)} %get-tuple-element.360), channel_id=1, source_target_pairs={{0,3},{1,4},{2,5},{3,6},{4,7},{5,0},{6,1},{7,2},{8,11},{9,12},{10,... | collective-permute-start | bytes 393224 | tf_op jit(solution)/shard_map/ppermute | solution.py:31
  84.6 46.9 %all-to-all-start.1 = ((bf16[16,8,4096]{2,1,0:T(8,128)(2,1)}), bf16[16,8,4096]{2,1,0:T(8,128)(2,1)}, u32[]{:S(2)}, u32[]{:S(2)}) async-start(bf16[16,8,4096]{2,1,0:T(8,128)(2,1)} %scatter_fusion.1), calls=%async_computation.1 | async-start | bytes 2097152 | tf_op jit(solution)/shard_map/all_to_all | solution.py:148
  97.3 188.2 %reduce-scatter.5.cloned.1.call-start = ((), (), s32[]{:S(2)}) async-start(), calls=%async_computation.7 | async-start | bytes 2359296 | tf_op jit(solution)/shard_map/reduce_scatter | solution.py:215
  157.5 60.0 %copy-start.6 = (s32[1,128]{1,0:T(1,128)S(1)}, s32[1,128]{1,0:T(1,128)}, u32[]{:S(2)}) copy-start(s32[1,128]{1,0:T(1,128)} %param.19) | copy-start | bytes 1540
  163.0 1.6 copy-start.1
  163.0 1.8 copy-start.2
  167.9 3.6 copy-start
  192.6 1.6 copy-start.1
  192.6 1.8 copy-start.2
  197.5 3.6 copy-start
  216.9 139.2 %reduce-scatter.3.cloned.1.call-start = ((), (), s32[]{:S(2)}) async-start(), calls=%async_computation.6 | async-start | bytes 2359296 | tf_op jit(solution)/shard_map/reduce_scatter | solution.py:214
Sparse Core Ops, SparseCore 0:
  10.2 57.0 all-gather.2
  69.4 57.8 all-gather.4
  217.1 68.4 reduce-scatter.4
  289.0 67.1 reduce-scatter.2
